TPU v7x, 128 devices: a whole 4x4x4 slice. The times are simulated.
128 devices in a mesh: aux: 8 (over y, core), depth: 4 (over z), blk: 4 (over x).
Axes of the slice: x: 4, y: 4, z: 4, core: 2. Of those that a mesh axis runs over, the one named last changes fastest.
Arguments:
- blocks: float32 [32, 32, 64, 64, 128], P(('aux', 'depth'), 'blk'), may hold values from -6 to 6
- pair_ids: int32 [32, 32], P(('aux', 'depth'), 'blk'), may hold values from 0 to 255, as said below
- counts: int32 [32, 4], P(('aux', 'depth'), 'blk'), may hold values from 1 to 8, as said below
- coeff: float32 [8, 1024], replicated, may hold values from -0.0034179688 to 0.0034179688
- domains: int32 [8, 24], replicated, may hold values from 0 to 31, as said below
Outputs:
- exchange: float32 [1024, 1024], P('blk', ('aux', 'depth'))
Inputs may be any that keep to these rules, and one draw needn't show every extreme that they name: `pair_ids`: within each list the ids are distinct, and the mu block of every id of the list of index k of blk lies in k * 4 to (k + 1) * 4 - 1. `counts`: slots at or past the count are not part of the list. `domains`: each row holds 24 distinct auxiliary block numbers.
All inputs are finite; a program needn't handle non-finite values.
Results may differ from a plain program's by a relative error of at most 0.0003.
Values sent between devices are 32-bit elements; how exact they have to be, the bound alone decides.
A program may use at most 64 MiB of HBM per device.

v0:
```python
import jax
import jax.numpy as jnp
from jax import lax
from jax.sharding import PartitionSpec as P

NB = 1024
BS = 64


def on_device(blocks, pair_ids, counts, coeff, domains):
    highest = lax.Precision.HIGHEST
    nblk = NB // BS
    per_dev = nblk // lax.axis_size("blk")
    group = blocks.shape[0]
    slots = blocks.shape[1]
    first_mu = lax.axis_index("blk") * per_dev
    valid = (jnp.arange(slots, dtype=jnp.int32)[None, :] < counts).astype(jnp.float32)
    nu_hot = (
        (pair_ids % nblk)[:, :, None] == jnp.arange(nblk, dtype=jnp.int32)[None, None, :]
    ).astype(jnp.float32)
    mu_hot = (
        (pair_ids // nblk - first_mu)[:, :, None]
        == jnp.arange(per_dev, dtype=jnp.int32)[None, None, :]
    ).astype(jnp.float32)
    mu_hot = mu_hot * valid[:, :, None]
    coeff_blocks = coeff.reshape(coeff.shape[0], nblk, BS)
    picked = jnp.einsum("asc,icn->asin", nu_hot, coeff_blocks, precision=highest)
    half = jnp.einsum("asmnq,asin->asqim", blocks, picked, precision=highest)
    placed = jnp.einsum("asb,asqim->aqibm", mu_hot, half, precision=highest)
    block_index = lax.axis_index(("aux", "depth")) * group + jnp.arange(group, dtype=jnp.int32)
    inside = jnp.any(domains[None, :, :] == block_index[:, None, None], axis=2).astype(jnp.float32)
    placed = placed * inside[:, None, :, None, None]
    local = placed.reshape(group * blocks.shape[4], coeff.shape[0], per_dev * BS)
    flat = local.reshape(-1, local.shape[2])
    piece = lax.all_gather(local, "blk", axis=2, tiled=True)
    columns = piece.reshape(-1, piece.shape[2])
    partial_k = lax.dot_general(flat, columns, (((0,), (0,)), ((), ())), precision=highest)
    owned = lax.psum_scatter(partial_k, ("aux", "depth"), scatter_dimension=1, tiled=True)
    return owned


def solution(mesh):
    placed = (
        P(("aux", "depth"), "blk", None, None, None),
        P(("aux", "depth"), "blk"),
        P(("aux", "depth"), "blk"),
        P(),
        P(),
    )
    return jax.shard_map(
        on_device, mesh=mesh, in_specs=placed, out_specs=P("blk", ("aux", "depth")), check_vma=False
    )
```

profile of v0, /device:TPU:0, one launch (start us, length us, event | category | flops | bytes accessed | tf_op | source)
XLA Modules:
  0.0 175.8 jit_solution(16511876811233065765)
XLA Ops:
  6.5 0.0 all-gather.2.cloned.1.call-start
  7.2 0.8 compare_reduce_fusion
  8.0 0.8 reshape.179
  8.9 0.7 subtract_bitcast_fusion
  9.5 0.2 convolution_bitcast_fusion
  9.7 10.7 %fusion.6 = f32[8,128,8,64]{1,2,3,0:T(8,128)S(1)} fusion(f32[1,8,64,64,128]{4,3,2,1,0:T(8,128)} %param.5, f32[8,8,64,1]{2,0,1,3:T(8,128)S(1)} %convolution_bitcast_fusion), kind=kOutput, calls=%fused_computation.6 | convolution fusion | flops 402653184 | bytes 18890752 | tf_op jit(solution)/shard_map/asmnq,asin->asqim/dot_general | solution.py:28
  20.4 3.0 %fusion.15 = f32[1,128,8,4,64]{1,3,4,2,0:T(4,128)S(1)} fusion(f32[8,128,8,64]{1,2,3,0:T(8,128)S(1)} %fusion.6, f32[8]{0:T(128)S(1)} %convert_element_type.21, f32[8]{0:T(128)S(1)} %compare_convert_fusion, s32[8]{0:T(128)S(1)} %get-tuple-element.5), kind=kOutput, calls=%fused_computation.9 | convolution fusion | flops 25428032 | bytes 3145824 | tf_op jit(solution)/shard_map/asb,asqim->aqibm/dot_general | solution.py:29
  23.4 1.1 copy.13
  24.5 0.0 all-gather.2.cloned.1.call-update
  24.6 0.2 reduce-scatter.2.cloned.1.call-start
  24.8 1.6 copy.12
  26.4 1.1 reshape_reshape.3
  27.5 47.9 %all-gather.2.cloned.1.call-done = f32[128,8,1024]{0,2,1:T(8,128)} async-done(((f32[128,8,256]{0,2,1:T(8,128)}), f32[128,8,1024]{0,2,1:T(8,128)}) %all-gather.2.cloned.1.call-update) | async-done | bytes 4194320 | tf_op jit(solution)/shard_map/all_gather | solution.py:35
  75.4 5.5 %copy.14 = f32[128,8,1024]{2,1,0:T(8,128)} copy(f32[128,8,1024]{0,2,1:T(8,128)} %all-gather.2.cloned.1.call-done) | data formatting | bytes 8388608 | tf_op jit(solution)/shard_map/all_gather | solution.py:35
  80.9 9.8 %fusion.2 = f32[256,1024]{0,1:T(8,128)} fusion(f32[1024,256]{1,0:T(8,128)S(1)} %reshape_reshape.3, f32[128,8,1024]{2,1,0:T(8,128)} %copy.14), kind=kOutput, calls=%fused_computation.2 | convolution fusion | flops 3221225472 | bytes 6291456 | tf_op jit(solution)/shard_map/dot_general | solution.py:37
  90.7 0.0 reduce-scatter.2.cloned.1.call-update
  90.8 78.2 %reduce-scatter.2.cloned.1.call-done = f32[256,32]{0,1:T(8,128)} async-done(((f32[256,1024]{0,1:T(8,128)}), f32[256,32]{0,1:T(8,128)}) %reduce-scatter.2.cloned.1.call-update) | async-done | bytes 32784 | tf_op jit(solution)/shard_map/reduce_scatter | solution.py:38
  (2 shorter events, 0.0 us)
Async XLA Ops:
  6.5 68.9 %all-gather.2.cloned.1.call-start = ((), (), s32[]{:S(2)}) async-start(), calls=%async_computation.1 | async-start | bytes 5242880 | tf_op jit(solution)/shard_map/all_gather | solution.py:35
  24.6 144.4 %reduce-scatter.2.cloned.1.call-start = ((), (), s32[]{:S(2)}) async-start(), calls=%async_computation.2 | async-start | bytes 1081344 | tf_op jit(solution)/shard_map/reduce_scatter | solution.py:38
Sparse Core Ops, SparseCore 0:
  24.7 50.6 all-gather.1
  90.9 78.0 reduce-scatter.1
where the time goes:
time: 176 us
  waiting for transfers between devices  126 us (72%)
  matrix products  23.7 us (13%)
  between operations  14.1 us (8%)
  local copies, waits for them, and re-layouts  10.2 us (6%)
    reduce_scatter x1, waiting for transfers between devices, on_device(): lax.psum_scatter(partial_k, ('aux', 'depth'), scatter_dimension=1, tiled=...  78.2 us
    all_gather x1, waiting for transfers between devices, on_device(): piece = lax.all_gather(local, 'blk', axis=2, tiled=True)  47.9 us
    dot_general x1, matrix products, on_device(): half = jnp.einsum('asmnq,asin->asqim', blocks, picked, precision=highest)  10.7 us
    dot_general x1, matrix products, on_device(): lax.dot_general(flat, columns, (((0,), (0,)), ((), ())), precision=highest)  9.85 us
    all_gather x1, local copies, waits for them, and re-layouts, on_device(): piece = lax.all_gather(local, 'blk', axis=2, tiled=True)  5.49 us
  transfers between devices with their start and end apart: 2, of which 2 were waited for; matrix products, arithmetic and copies ran while one was open for 2% of the time, Pallas kernels for 0%

commit v1 on v0

v1 whole, which is shorter than its diff:
```python
import functools

import jax
import jax.numpy as jnp
from jax import lax
from jax.experimental import pallas as pl
from jax.experimental.pallas import tpu as pltpu
from jax.sharding import PartitionSpec as P

MESH = pl.DeviceIdType.MESH
F32, BF16 = jnp.float32, jnp.bfloat16
T = 4


def split(v):
    hi = v.astype(BF16)
    return hi, (v - hi.astype(F32)).astype(BF16)


def dot(a, b, contract):
    return lax.dot_general(a, b, ((contract[0], contract[1]), ((), ())), preferred_element_type=F32)


def kernel(ids, cnt, coeff, domains, blocks, out,
           buf, w, fs, g, gs, yb, s0, s1, r0, r1, a0, a1, b0, b1, xs, xr,
           h_sem, l_sem, x_snd, x_rcv, c_snd, c_rcv, p_snd, p_rcv, q_snd, q_rcv, f_snd, f_rcv):
    aux = lax.axis_index("aux")
    z = lax.axis_index("depth")
    x = lax.axis_index("blk")
    y, c = aux // 2, aux % 2

    def at_x(d):
        return {"blk": (x + d) % 4}

    def at_y(d):
        return {"aux": ((y + d) % 4) * 2 + c}

    def at_z(d):
        return {"depth": (z + d) % 4}

    sibling = {"aux": y * 2 + (1 - c)}

    loads = []
    for t in range(T):
        for h in range(2):
            rows = pl.ds(32 * h + 8 * t, 8)
            cp = pltpu.make_async_copy(blocks.at[0, :, rows], buf.at[:, rows], h_sem.at[t, h])
            cp.start()
            loads.append(cp)

    barrier = pltpu.get_barrier_semaphore()
    for d in (1, 2, 3):
        for to in (at_x(d), at_y(d), at_z(d)):
            pl.semaphore_signal(barrier, inc=1, device_id=to, device_id_type=MESH)
    pl.semaphore_signal(barrier, inc=1, device_id=sibling, device_id_type=MESH)

    index = aux * 4 + z
    inside = jnp.max(jnp.where(domains[...] == index, 1.0, 0.0), axis=1, keepdims=True)
    lane = lax.broadcasted_iota(jnp.int32, (64, 512), 1)
    pair = jnp.full((64, 512), -1, jnp.int32)
    for s in range(8):
        here = jnp.where(s < cnt[...], ids[:, s:s + 1], -1)
        pair = jnp.where(lane // 64 == s, here, pair)
    mu = jnp.where(pair >= 0, pair // 16 - 4 * x, -1)
    nu = jnp.where(pair >= 0, pair % 16, -1)[:8]
    low = lax.broadcasted_iota(jnp.int32, (8, 128), 1) < 64
    picked = jnp.zeros((8, 512), F32)
    for u in range(8):
        two = coeff[:, 128 * u:128 * u + 128]
        turned = pltpu.roll(two, 64, axis=1)
        for e, wide in enumerate((jnp.where(low, two, turned), jnp.where(low, turned, two))):
            picked = jnp.where(nu == 2 * u + e, jnp.concatenate([wide] * 4, axis=1), picked)
    picked = picked * inside
    hi, lo = split(picked)
    both = jnp.concatenate([hi.astype(F32), lo.astype(F32)], axis=0).astype(BF16)
    row = lax.broadcasted_iota(jnp.int32, (64, 16), 0)
    col = lax.broadcasted_iota(jnp.int32, (64, 16), 1)
    spread = jnp.where(row // 4 == col, 1.0, 0.0).astype(BF16)
    wide = dot(spread, both, ((1,), (0,)))
    brow = lax.broadcasted_iota(jnp.int32, (64, 512), 0) % 4
    w[...] = jnp.where(brow == mu, wide, 0.0).astype(BF16)

    x_copies = []
    l_copies = []
    for t in range(T):
        for h in range(2):
            loads[2 * t + h].wait()

            def pair_of_m(p, carry, t=t, h=h):
                m0 = 32 * h + 8 * t + 2 * p
                tiles = [buf[:, m0 + e].reshape(512, 128) for e in range(2)]
                bhi, blo = split(jnp.concatenate(tiles, axis=1))
                one = dot(w[...], bhi, ((1,), (0,)))
                res = one[:32] + one[32:] + dot(w[:32], blo, ((1,), (0,)))
                for e in range(2):
                    for j in range(4):
                        for i in range(2):
                            r = 8 * j + 4 * i
                            fs[t, j, i, pl.ds(8 * h + 2 * p + e, 4, stride=16), :] = res[r:r + 4, 128 * e:128 * e + 128]
                return carry

            lax.fori_loop(0, 4, pair_of_m, 0)
        if t == 0:
            pl.semaphore_wait(barrier, 10)
        for d in (1, 2, 3):
            cp = pltpu.make_async_remote_copy(
                src_ref=fs.at[t, (x + d) % 4], dst_ref=g.at[t, x], send_sem=x_snd.at[t, d - 1], recv_sem=x_rcv.at[t, d - 1],
                device_id=at_x(d), device_id_type=MESH)
            cp.start()
            x_copies.append(cp)
        cp = pltpu.make_async_copy(fs.at[t, x], g.at[t, x], l_sem.at[t])
        cp.start()
        l_copies.append(cp)

    def keep(src, t, base):
        for i in range(2):
            hi, lo = split(src[t, :, i].reshape(256, 128))
            yb[t, :, pl.ds(base + 128 * i, 128)] = hi
            yb[t, :, pl.ds(512 + base + 128 * i, 128)] = lo

    def block(tr, tc, at):
        left = jnp.concatenate([yb[tr, pl.ds(pl.multiple_of(64 * k + 32 * c, 32), 32), :] for k in range(4)], axis=0)
        right = yb[tc]
        con = ((1,), (1,))
        res = dot(left[:, :512], right[:, :512], con)
        res += dot(left[:, :512], right[:, 512:], con)
        res += dot(left[:, 512:], right[:, :512], con)
        for ky in range(4):
            for zz in range(4):
                r = 32 * ky + 8 * zz
                s0[zz, at, ky] = res[r:r + 8, :128]
                s1[ky, at, zz] = res[r:r + 8, 128:]

    def first(t):
        n = pl.ds(t * t, 2 * t + 1)
        cps = []
        for d in (1, 2, 3):
            cp0 = pltpu.make_async_remote_copy(
                src_ref=s0.at[(z + d) % 4, n], dst_ref=r0.at[d - 1, n], send_sem=p_snd.at[0, t, d - 1], recv_sem=p_rcv.at[0, t, d - 1],
                device_id=at_z(d), device_id_type=MESH)
            cp1 = pltpu.make_async_remote_copy(
                src_ref=s1.at[(y + d) % 4, n], dst_ref=r1.at[d - 1, n], send_sem=p_snd.at[1, t, d - 1], recv_sem=p_rcv.at[1, t, d - 1],
                device_id=at_y(d), device_id_type=MESH)
            cp0.start()
            cp1.start()
            cps += [cp0, cp1]
        return cps

    def second(t, cps):
        n = pl.ds(t * t, 2 * t + 1)
        for cp in cps:
            cp.wait_recv()
        for own, s, r, a in ((z, s0, r0, a0), (y, s1, r1, a1)):
            tot = s[own, n] + r[0, n] + r[1, n] + r[2, n]
            for k in range(4):
                a[k, n] = tot[:, k]
        new = []
        for d in (1, 2, 3):
            cp0 = pltpu.make_async_remote_copy(
                src_ref=a0.at[(y + d) % 4, n], dst_ref=b0.at[d - 1, n], send_sem=q_snd.at[0, t, d - 1], recv_sem=q_rcv.at[0, t, d - 1],
                device_id=at_y(d), device_id_type=MESH)
            cp1 = pltpu.make_async_remote_copy(
                src_ref=a1.at[(z + d) % 4, n], dst_ref=b1.at[d - 1, n], send_sem=q_snd.at[1, t, d - 1], recv_sem=q_rcv.at[1, t, d - 1],
                device_id=at_z(d), device_id_type=MESH)
            cp0.start()
            cp1.start()
            new += [cp0, cp1]
        return new

    one_copies, two_copies, sib_copies = [], [], []
    for t in range(T):
        for cp in x_copies[3 * t:3 * t + 3]:
            cp.wait_recv()
        l_copies[t].wait()
        cp = pltpu.make_async_remote_copy(
            src_ref=g.at[t], dst_ref=gs.at[t], send_sem=c_snd.at[t], recv_sem=c_rcv.at[t], device_id=sibling, device_id_type=MESH)
        cp.start()
        sib_copies.append(cp)
        keep(g, t, 0)
        cp.wait_recv()
        keep(gs, t, 256)
        for tc in range(t + 1):
            block(t, tc, t * t + tc)
        for tr in range(t):
            block(tr, t, t * t + t + 1 + tr)
        one_copies.append(first(t))
        if t >= 1:
            two_copies.append(second(t - 1, one_copies[t - 1]))
    two_copies.append(second(T - 1, one_copies[T - 1]))

    for cps in two_copies:
        for cp in cps:
            cp.wait_recv()
    done = [a0[y] + b0[0] + b0[1] + b0[2], a1[z] + b1[0] + b1[1] + b1[2]]

    def place(tr, tc):
        return tr * tr + tc if tr >= tc else tc * tc + tc + 1 + tr

    for f in range(2):
        for tr in range(T):
            for u in range(2):
                even, odd = done[f][place(tr, 2 * u)], done[f][place(tr, 2 * u + 1)]
                xs[2 * f, tr, u] = jnp.where(low, even, pltpu.roll(odd, 64, axis=1))
                xs[2 * f + 1, tr, u] = jnp.where(low, pltpu.roll(even, 64, axis=1), odd)
    last = []
    for d in (1, 2, 3):
        cp = pltpu.make_async_remote_copy(
            src_ref=xs.at[(x + d) % 4], dst_ref=xr.at[d - 1], send_sem=f_snd.at[d - 1], recv_sem=f_rcv.at[d - 1],
            device_id=at_x(d), device_id_type=MESH)
        cp.start()
        last.append(cp)
    for cp in last:
        cp.wait_recv()
    total = xs[x] + xr[0] + xr[1] + xr[2]
    for u in range(2):
        turned = total[:, u].reshape(32, 128).T
        for e in range(2):
            for b in range(4):
                for h in range(2):
                    r = 64 * e + 16 * b + 8 * h
                    out[pl.ds(64 * b + 32 * h + 8 * (2 * u + e), 8), :] = turned[r:r + 8, :]
    for cp in x_copies + sib_copies + last:
        cp.wait_send()
    for cps in one_copies + two_copies:
        for cp in cps:
            cp.wait_send()


def on_device(blocks, pair_ids, counts, coeff, domains):
    vmem = pl.BlockSpec(memory_space=pltpu.VMEM)
    dma = pltpu.SemaphoreType.DMA
    return pl.pallas_call(
        kernel,
        out_shape=jax.ShapeDtypeStruct((256, 32), F32),
        in_specs=[vmem, vmem, vmem, vmem, pl.BlockSpec(memory_space=pl.ANY)],
        out_specs=vmem,
        scratch_shapes=[
            pltpu.VMEM((8, 64, 64, 128), F32),
            pltpu.VMEM((64, 512), BF16),
            pltpu.VMEM((T, 4, 2, 64, 128), F32),
            pltpu.VMEM((T, 4, 2, 64, 128), F32),
            pltpu.VMEM((T, 4, 2, 64, 128), F32),
            pltpu.VMEM((T, 256, 1024), BF16),
            pltpu.VMEM((4, 16, 4, 8, 128), F32),
            pltpu.VMEM((4, 16, 4, 8, 128), F32),
            pltpu.VMEM((3, 16, 4, 8, 128), F32),
            pltpu.VMEM((3, 16, 4, 8, 128), F32),
            pltpu.VMEM((4, 16, 8, 128), F32),
            pltpu.VMEM((4, 16, 8, 128), F32),
            pltpu.VMEM((3, 16, 8, 128), F32),
            pltpu.VMEM((3, 16, 8, 128), F32),
            pltpu.VMEM((4, 4, 2, 8, 128), F32),
            pltpu.VMEM((3, 4, 2, 8, 128), F32),
            dma((T, 2)), dma((T,)),
            dma((T, 3)), dma((T, 3)),
            dma((T,)), dma((T,)),
            dma((2, T, 3)), dma((2, T, 3)),
            dma((2, T, 3)), dma((2, T, 3)),
            dma((3,)), dma((3,)),
        ],
        compiler_params=pltpu.CompilerParams(
            collective_id=0, has_side_effects=True, vmem_limit_bytes=48 * 2**20),
    )(pair_ids, counts, coeff, domains, blocks)


def solution(mesh):
    placed = (
        P(("aux", "depth"), "blk", None, None, None),
        P(("aux", "depth"), "blk"),
        P(("aux", "depth"), "blk"),
        P(),
        P(),
    )
    return jax.shard_map(
        on_device, mesh=mesh, in_specs=placed, out_specs=P("blk", ("aux", "depth")), check_vma=False
    )
```

time: 176 us -> 47.8 us (0.27)
  waiting for transfers between devices: 126 us -> 0 us
  Pallas kernels: 0 us -> 44.1 us
  matrix products: 23.7 us -> 0 us
  between operations: 14.1 us -> 0.67 us
  local copies, waits for them, and re-layouts: 10.2 us -> 2.78 us
    reduce_scatter x1 -> x0, waiting for transfers between devices: 78.2 us -> none  [on_device(): lax.psum_scatter(partial_k, ('aux', 'depth'), scatter_dimension=1, tiled=...]
    all_gather x1 -> x0, waiting for transfers between devices: 47.9 us -> none  [on_device(): piece = lax.all_gather(local, 'blk', axis=2, tiled=True)]
    pallas_call x0 -> x1, Pallas kernels: none -> 44.1 us  [on_device(): pl.pallas_call(kernel, out_shape=jax.ShapeDtypeStruct((256, 32), F32), in...]
    dot_general x4 -> x0, matrix products: 23.7 us -> none  [the longest x1 10.7 us: on_device(): half = jnp.einsum('asmnq,asin->asqim', blocks, picked, precision=highest)]
    all_gather x1 -> x0, local copies, waits for them, and re-layouts: 5.49 us -> none  [on_device(): piece = lax.all_gather(local, 'blk', axis=2, tiled=True)]
    mul x2 -> x0, local copies, waits for them, and re-layouts: 2.7 us -> none  [on_device(): placed = placed * inside[:, None, :, None, None]]
    unnamed x0 -> x6, local copies, waits for them, and re-layouts: none -> 2.09 us
  transfers between devices with their start and end apart: 2 -> 0, of which waited for: 2 -> 0; matrix products, arithmetic and copies ran while one was open for 2% -> 0% of each run, Pallas kernels for 0% -> 0%
where the time goes in v1:
time: 47.8 us; the launch traced here: 47.6 us
  Pallas kernels  44.1 us (92%)
  local copies, waits for them, and re-layouts  2.78 us (6%)
  between operations  0.67 us (1%)
    pallas_call x1, Pallas kernels, on_device(): pl.pallas_call(kernel, out_shape=jax.ShapeDtypeStruct((256, 32), F32), in...  44.1 us
    unnamed x6, local copies, waits for them, and re-layouts  2.09 us

profile of v1, /device:TPU:0, one launch (start us, length us, event | category | flops | bytes accessed | tf_op | source)
XLA Modules:
  0.0 47.6 jit_solution(11674537851813365662)
XLA Ops:
  0.7 0.0 copy-start
  0.7 0.7 %copy-done = f32[8,1024]{1,0:T(8,128)S(1)} copy-done((f32[8,1024]{1,0:T(8,128)S(1)}, f32[8,1024]{1,0:T(8,128)}, u32[]{:S(2)}) %copy-start) | copy-done | bytes 32792
  1.4 0.0 copy-start.1
  1.4 0.7 %copy-done.1 = s32[8,24]{1,0:T(8,128)S(1)} copy-done((s32[8,24]{1,0:T(8,128)S(1)}, s32[8,24]{1,0:T(8,128)}, u32[]{:S(2)}) %copy-start.1) | copy-done | bytes 792
  2.1 0.0 copy-start.2
  2.1 0.7 %copy-done.2 = s32[1,8]{1,0:T(1,128)S(1)} copy-done((s32[1,8]{1,0:T(1,128)S(1)}, s32[1,8]{1,0:T(1,128)}, u32[]{:S(2)}) %copy-start.2) | copy-done | bytes 56
  2.8 44.1 %shard_map.55 = f32[256,32]{1,0:T(8,128)S(1)} custom-call(s32[1,8]{1,0:T(1,128)S(1)} %copy-done.2, s32[1,1]{1,0:T(1,128)S(6)} %copy.7.cnt, f32[8,1024]{1,0:T(8,128)S(1)} %copy-done, s32[8,24]{1,0:T(8,128)S(1)} %copy-done.1, f32[1,8,64,64,128]{4,3,2,1,0:T(8,128)} %blocks.1), custom_call_target="tpu_custom_call" | custom-call | tf_op jit(solution)/shard_map/pallas_call | solution.py:232
  46.9 0.7 %copy.6 = f32[256,32]{0,1:T(8,128)} copy(f32[256,32]{1,0:T(8,128)S(1)} %shard_map.55) | data formatting | bytes 65536 | tf_op jit(solution)/shard_map/pallas_call | solution.py:232
Async XLA Ops:
  0.7 0.8 %copy-start = (f32[8,1024]{1,0:T(8,128)S(1)}, f32[8,1024]{1,0:T(8,128)}, u32[]{:S(2)}) copy-start(f32[8,1024]{1,0:T(8,128)} %coeff.1) | copy-start | bytes 98308
  1.4 0.7 %copy-start.1 = (s32[8,24]{1,0:T(8,128)S(1)}, s32[8,24]{1,0:T(8,128)}, u32[]{:S(2)}) copy-start(s32[8,24]{1,0:T(8,128)} %domains.1) | copy-start | bytes 2308
  2.1 0.7 %copy-start.2 = (s32[1,8]{1,0:T(1,128)S(1)}, s32[1,8]{1,0:T(1,128)}, u32[]{:S(2)}) copy-start(s32[1,8]{1,0:T(1,128)} %ids.1) | copy-start | bytes 100

commit v2 on v0

v2 whole, which is shorter than its diff:
```python
import jax
import jax.numpy as jnp
from jax import lax
from jax.experimental import pallas as pl
from jax.experimental.pallas import tpu as pltpu
from jax.sharding import PartitionSpec as P

MESH = pl.DeviceIdType.MESH
F32, BF16 = jnp.float32, jnp.bfloat16
T = 4
AHEAD = 3
GROUPS = ((0, "all"), (1, "all"), (2, "all"), (3, "columns"), (3, "rows"))


def split(v):
    hi = v.astype(BF16)
    return hi, (v - hi.astype(F32)).astype(BF16)


def dot(a, b, contract):
    return lax.dot_general(a, b, ((contract[0], contract[1]), ((), ())), preferred_element_type=F32)


def span(group):
    t, kind = GROUPS[group]
    if kind == "columns":
        return t * t, t
    if kind == "rows":
        return t * t + t, t + 1
    return t * t, 2 * t + 1


def kernel(ids_in, cnt_in, coeff_in, domains_in, blocks, out,
           ids, cnt, coeff, domains, buf, w, fs, g, gs, rh, rl, lh, s0, s1, r0, r1, a0, a1, b0, b1, xs, xr,
           i_sem, h_sem, l_sem, x_snd, x_rcv, c_snd, c_rcv, p_snd, p_rcv, q_snd, q_rcv, f_snd, f_rcv):
    aux = lax.axis_index("aux")
    z = lax.axis_index("depth")
    x = lax.axis_index("blk")
    y, c = aux // 2, aux % 2

    def at_x(d):
        return {"blk": (x + d) % 4}

    def at_y(d):
        return {"aux": ((y + d) % 4) * 2 + c}

    def at_z(d):
        return {"depth": (z + d) % 4}

    sibling = {"aux": y * 2 + (1 - c)}

    def send(src, dst, snd, rcv, to):
        cp = pltpu.make_async_remote_copy(
            src_ref=src, dst_ref=dst, send_sem=snd, recv_sem=rcv, device_id=to, device_id_type=MESH)
        cp.start()
        return cp

    def await_bytes(ref, sem):
        pltpu.make_async_copy(ref, ref, sem).wait()

    barrier = pltpu.get_barrier_semaphore()
    for d in (2, 1, 3):
        for to in (at_z(d), at_x(d), at_y(d)):
            pl.semaphore_signal(barrier, inc=1, device_id=to, device_id_type=MESH)
    pl.semaphore_signal(barrier, inc=1, device_id=sibling, device_id_type=MESH)

    small = []
    for k, (src, dst) in enumerate(((ids_in, ids), (cnt_in, cnt), (coeff_in, coeff), (domains_in, domains))):
        small.append(pltpu.make_async_copy(src, dst, i_sem.at[k]))
        small[-1].start()
    loads = []
    for t in range(T):
        for h in range(2):
            rows = pl.ds(32 * h + 8 * t, 8)
            loads.append(pltpu.make_async_copy(blocks.at[0, :, rows], buf.at[:, rows], h_sem.at[t, h]))
    for cp in loads[:AHEAD]:
        cp.start()
    for cp in small:
        cp.wait()

    index = aux * 4 + z
    inside = jnp.max(jnp.where(domains[...] == index, 1.0, 0.0), axis=1, keepdims=True)
    lane = lax.broadcasted_iota(jnp.int32, (64, 512), 1)
    pair = jnp.full((64, 512), -1, jnp.int32)
    for s in range(8):
        here = jnp.where(s < cnt[...], ids[:, s:s + 1], -1)
        pair = jnp.where(lane // 64 == s, here, pair)
    mu = jnp.where(pair >= 0, pair // 16 - 4 * x, -1)
    nu = jnp.where(pair >= 0, pair % 16, -1)[:8]
    low = lax.broadcasted_iota(jnp.int32, (8, 128), 1) < 64
    picked = jnp.zeros((8, 512), F32)
    for u in range(8):
        two = coeff[:, 128 * u:128 * u + 128]
        turned = pltpu.roll(two, 64, axis=1)
        for e, wide in enumerate((jnp.where(low, two, turned), jnp.where(low, turned, two))):
            picked = jnp.where(nu == 2 * u + e, jnp.concatenate([wide] * 4, axis=1), picked)
    picked = picked * inside
    hi, lo = split(picked)
    both = jnp.concatenate([hi.astype(F32), lo.astype(F32)], axis=0).astype(BF16)
    row = lax.broadcasted_iota(jnp.int32, (64, 16), 0)
    col = lax.broadcasted_iota(jnp.int32, (64, 16), 1)
    spread = jnp.where(row // 4 == col, 1.0, 0.0).astype(BF16)
    wide = dot(spread, both, ((1,), (0,)))
    brow = lax.broadcasted_iota(jnp.int32, (64, 512), 0) % 4
    w[...] = jnp.where(brow == mu, wide, 0.0).astype(BF16)

    x_copies, l_copies = [], []
    for t in range(T):
        for h in range(2):
            loads[2 * t + h].wait()
            if 2 * t + h + AHEAD < len(loads):
                loads[2 * t + h + AHEAD].start()

            def pair_of_m(p, carry, t=t, h=h):
                m0 = 32 * h + 8 * t + 2 * p
                tiles = [buf[:, m0 + e].reshape(512, 128) for e in range(2)]
                bhi, blo = split(jnp.concatenate(tiles, axis=1))
                one = dot(w[...], bhi, ((1,), (0,)))
                res = one[:32] + one[32:] + dot(w[:32], blo, ((1,), (0,)))
                for e in range(2):
                    for j in range(4):
                        for i in range(2):
                            r = 8 * j + 4 * i
                            fs[t, j, i, pl.ds(8 * h + 2 * p + e, 4, stride=16), :] = res[r:r + 4, 128 * e:128 * e + 128]
                return carry

            lax.fori_loop(0, 4, pair_of_m, 0)
        if t == 0:
            pl.semaphore_wait(barrier, 10)
        for d in (2, 1, 3):
            x_copies.append(send(fs.at[t, (x + d) % 4], g.at[t, x], x_snd, x_rcv.at[t, d - 1], at_x(d)))
        send(fs.at[t, x], gs.at[t, x], c_snd, c_rcv.at[t], sibling)
        cp = pltpu.make_async_copy(fs.at[t, x], g.at[t, x], l_sem.at[t])
        cp.start()
        l_copies.append(cp)

    def keep(src, t, k, base):
        for i in range(2):
            lanes = pl.ds(base + 128 * i, 128)
            rows = pl.ds(pl.multiple_of(64 * k, 64), 64)
            hi, lo = split(src[t, k, i])
            rh[t, rows, lanes] = hi
            rl[t, rows, lanes] = lo
            hi, lo = split(src[t, k, i, pl.ds(pl.multiple_of(32 * c, 32), 32)])
            lh[t, pl.ds(pl.multiple_of(32 * k, 32), 32), lanes] = hi
            lh[t, pl.ds(pl.multiple_of(128 + 32 * k, 32), 32), lanes] = lo

    con = ((1,), (1,))

    def store(res, at):
        for ky in range(4):
            for zz in range(4):
                r = 32 * ky + 8 * zz
                s0[zz, at, ky] = res[r:r + 8, :128]
                s1[ky, at, zz] = res[r:r + 8, 128:]

    def columns(t):
        big = dot(lh[:t].reshape(256 * t, 512), rh[t], con)
        add = dot(jnp.concatenate([lh[u, :128] for u in range(t)], axis=0), rl[t], con)
        for u in range(t):
            res = big[256 * u:256 * u + 128] + big[256 * u + 128:256 * u + 256] + add[128 * u:128 * u + 128]
            store(res, t * t + u)

    def rows(t):
        for u in range(t + 1):
            big = dot(lh[t], rh[u], con)
            store(big[:128] + big[128:] + dot(lh[t, :128], rl[u], con), t * t + t + u)

    def first(k):
        n = pl.ds(*span(k))
        for d in (2, 1, 3):
            send(s0.at[(z + d) % 4, n], r0.at[d - 1, n], p_snd.at[0], p_rcv.at[0, k], at_z(d))
            send(s1.at[(y + d) % 4, n], r1.at[d - 1, n], p_snd.at[1], p_rcv.at[1, k], at_y(d))

    def second(k):
        n = pl.ds(*span(k))
        for f, (own, s, r, a, b, to, me) in enumerate(
                ((z, s0, r0, a0, b0, at_y, y), (y, s1, r1, a1, b1, at_z, z))):
            await_bytes(r.at[:, n], p_rcv.at[f, k])
            tot = s[own, n] + r[0, n] + r[1, n] + r[2, n]
            for u in range(4):
                a[u, n] = tot[:, u]
            for d in (2, 1, 3):
                send(a.at[(me + d) % 4, n], b.at[d - 1, n], q_snd.at[f], q_rcv.at[f, k], to(d))

    ready = 0
    for t in range(T):
        l_copies[t].wait()
        keep(g, t, x, 0)
        for d in (1, 3, 2):
            x_copies[3 * t + (2, 1, 3).index(d)].wait_recv()
            k = (x - d + 4) % 4
            send(g.at[t, k], gs.at[t, k], c_snd, c_rcv.at[t], sibling)
            keep(g, t, k, 0)
        await_bytes(gs.at[t], c_rcv.at[t])
        for k in range(4):
            keep(gs, t, k, 256)
        if t > 0:
            columns(t)
        if t == T - 1:
            first(3)
        rows(t)
        first(min(t, 3) + (t == T - 1))
        if t > 0:
            second(t - 1)
    second(3)
    second(4)

    done = []
    for f, (a, b, me) in enumerate(((a0, b0, y), (a1, b1, z))):
        for k in range(len(GROUPS)):
            await_bytes(b.at[:, pl.ds(*span(k))], q_rcv.at[f, k])
        done.append(a[me] + b[0] + b[1] + b[2])

    def place(tr, tc):
        return tr * tr + tr + tc if tr >= tc else tc * tc + tr

    for f in range(2):
        for tr in range(T):
            for u in range(2):
                even, odd = done[f][place(tr, 2 * u)], done[f][place(tr, 2 * u + 1)]
                xs[2 * f, tr, u] = jnp.where(low, even, pltpu.roll(odd, 64, axis=1))
                xs[2 * f + 1, tr, u] = jnp.where(low, pltpu.roll(even, 64, axis=1), odd)
    for d in (2, 1, 3):
        send(xs.at[(x + d) % 4], xr.at[d - 1], f_snd, f_rcv, at_x(d))
    await_bytes(xr, f_rcv)
    total = xs[x] + xr[0] + xr[1] + xr[2]
    pieces = {}
    for u in range(2):
        turned = total[:, u].reshape(32, 128).T
        for e in range(2):
            for b in range(4):
                for h in range(2):
                    r = 64 * e + 16 * b + 8 * h
                    pieces[b, h, 2 * u + e] = turned[r:r + 8]
    for half in range(2):
        cols = jnp.concatenate([pieces[k] for k in sorted(pieces) if k[0] // 2 == half], axis=0)
        out[:, 128 * half:128 * half + 128] = cols.T
    await_bytes(fs.at[:, :3], x_snd)
    await_bytes(gs, c_snd)
    for f, (r, b) in enumerate(((r0, b0), (r1, b1))):
        await_bytes(r, p_snd.at[f])
        await_bytes(b, q_snd.at[f])
    await_bytes(xr, f_snd)


def hold(v):
    return pltpu.with_memory_space_constraint(v, pltpu.HBM)


def on_device(blocks, pair_ids, counts, coeff, domains):
    hbm = pl.BlockSpec(memory_space=pltpu.HBM)
    dma = pltpu.SemaphoreType.DMA
    vmem = pltpu.VMEM
    cols = pl.pallas_call(
        kernel,
        out_shape=jax.ShapeDtypeStruct((32, 256), F32),
        in_specs=[hbm] * 5,
        out_specs=pl.BlockSpec(memory_space=vmem),
        scratch_shapes=[
            vmem((1, 8), jnp.int32), vmem((1, 1), jnp.int32), vmem((8, 1024), F32), vmem((8, 24), jnp.int32),
            vmem((8, 64, 64, 128), F32),
            vmem((64, 512), BF16),
            vmem((T, 4, 2, 64, 128), F32),
            vmem((T, 4, 2, 64, 128), F32),
            vmem((T, 4, 2, 64, 128), F32),
            vmem((T, 256, 512), BF16),
            vmem((T, 256, 512), BF16),
            vmem((T, 256, 512), BF16),
            vmem((4, 16, 4, 8, 128), F32),
            vmem((4, 16, 4, 8, 128), F32),
            vmem((3, 16, 4, 8, 128), F32),
            vmem((3, 16, 4, 8, 128), F32),
            vmem((4, 16, 8, 128), F32),
            vmem((4, 16, 8, 128), F32),
            vmem((3, 16, 8, 128), F32),
            vmem((3, 16, 8, 128), F32),
            vmem((4, 4, 2, 8, 128), F32),
            vmem((3, 4, 2, 8, 128), F32),
            dma((4,)), dma((T, 2)), dma((T,)),
            dma, dma((T, 3)),
            dma, dma((T,)),
            dma((2,)), dma((2, len(GROUPS))),
            dma((2,)), dma((2, len(GROUPS))),
            dma, dma,
        ],
        compiler_params=pltpu.CompilerParams(
            collective_id=0, has_side_effects=True, vmem_limit_bytes=VMEM_LIMIT),
    )(hold(pair_ids), counts, hold(coeff), hold(domains), blocks)
    return cols.T


VMEM_LIMIT = 48 * 2**20


def solution(mesh):
    placed = (
        P(("aux", "depth"), "blk", None, None, None),
        P(("aux", "depth"), "blk"),
        P(("aux", "depth"), "blk"),
        P(),
        P(),
    )
    return jax.shard_map(
        on_device, mesh=mesh, in_specs=placed, out_specs=P("blk", ("aux", "depth")), check_vma=False
    )
```

time: 176 us -> 43.4 us (0.25)
  waiting for transfers between devices: 126 us -> 0 us
  Pallas kernels: 0 us -> 42.1 us
  matrix products: 23.7 us -> 0 us
  between operations: 14.1 us -> 0.66 us
  local copies, waits for them, and re-layouts: 10.2 us -> 0.62 us
    reduce_scatter x1 -> x0, waiting for transfers between devices: 78.2 us -> none  [on_device(): lax.psum_scatter(partial_k, ('aux', 'depth'), scatter_dimension=1, tiled=...]
    all_gather x1 -> x0, waiting for transfers between devices: 47.9 us -> none  [on_device(): piece = lax.all_gather(local, 'blk', axis=2, tiled=True)]
    pallas_call x0 -> x1, Pallas kernels: none -> 42.1 us  [on_device(): pl.pallas_call(kernel, out_shape=jax.ShapeDtypeStruct((32, 256), F32), in...]
    dot_general x4 -> x0, matrix products: 23.7 us -> none  [the longest x1 10.7 us: on_device(): half = jnp.einsum('asmnq,asin->asqim', blocks, picked, precision=highest)]
    all_gather x1 -> x0, local copies, waits for them, and re-layouts: 5.49 us -> none  [on_device(): piece = lax.all_gather(local, 'blk', axis=2, tiled=True)]
    mul x2 -> x0, local copies, waits for them, and re-layouts: 2.7 us -> none  [on_device(): placed = placed * inside[:, None, :, None, None]]
  transfers between devices with their start and end apart: 2 -> 0, of which waited for: 2 -> 0; matrix products, arithmetic and copies ran while one was open for 2% -> 0% of each run, Pallas kernels for 0% -> 0%
where the time goes in v2:
time: 43.4 us; the launch traced here: 43.3 us
  Pallas kernels  42.1 us (97%)
  between operations  0.66 us (2%)
  local copies, waits for them, and re-layouts  0.62 us (1%)
    pallas_call x1, Pallas kernels, on_device(): pl.pallas_call(kernel, out_shape=jax.ShapeDtypeStruct((32, 256), F32), in...  42.1 us

profile of v2, /device:TPU:0, one launch (start us, length us, event | category | flops | bytes accessed | tf_op | source)
XLA Modules:
  0.0 43.3 jit_solution(18427803583681970885)
XLA Ops:
  0.7 42.1 %shard_map.55 = f32[32,256]{1,0:T(8,128)S(1)} custom-call(s32[1,8]{1,0:T(1,128)} %ids_in.1, s32[1,1]{1,0:T(1,128)S(6)} %copy.7.cnt_in, f32[8,1024]{1,0:T(8,128)} %coeff_in.1, s32[8,24]{1,0:T(8,128)} %domains_in.1, f32[1,8,64,64,128]{4,3,2,1,0:T(8,128)} %blocks.1), custom_call_target="tpu_custom_call" | custom-call | tf_op jit(solution)/shard_map/pallas_call | solution.py:255
  42.7 0.6 %copy.8 = f32[256,32]{0,1:T(8,128)} copy(f32[256,32]{0,1:T(8,128)S(1)} %bitcast.1) | data formatting | bytes 65536

commit v3 on v2

--- a/solution.py
+++ b/solution.py
@@ -8,8 +8,18 @@
 MESH = pl.DeviceIdType.MESH
 F32, BF16 = jnp.float32, jnp.bfloat16
 T = 4
-AHEAD = 3
-GROUPS = ((0, "all"), (1, "all"), (2, "all"), (3, "columns"), (3, "rows"))
+AHEAD = 2
+GROUPS = (
+    ((0, 0),),
+    ((0, 1), (1, 0), (1, 1)),
+    ((0, 2), (1, 2), (2, 0), (2, 1), (2, 2)),
+    ((0, 3), (1, 3), (2, 3)),
+)
+PLACE = {pair: at for at, pair in enumerate(sum(GROUPS, ()))}
+NB = len(PLACE)
+STEPWISE = (0, 1, 2)
+NQ = sum(len(GROUPS[k]) for k in STEPWISE)
+PAIRS = (((0, 0), (0, 1)), ((1, 0), (1, 1)), ((2, 0), (2, 1)), ((0, 2), (1, 2)), ((2, 2),))
 
 
 def split(v):
@@ -22,17 +32,12 @@
 
 
 def span(group):
-    t, kind = GROUPS[group]
-    if kind == "columns":
-        return t * t, t
-    if kind == "rows":
-        return t * t + t, t + 1
-    return t * t, 2 * t + 1
+    return PLACE[GROUPS[group][0]], len(GROUPS[group])
 
 
 def kernel(ids_in, cnt_in, coeff_in, domains_in, blocks, out,
-           ids, cnt, coeff, domains, buf, w, fs, g, gs, rh, rl, lh, s0, s1, r0, r1, a0, a1, b0, b1, xs, xr,
-           i_sem, h_sem, l_sem, x_snd, x_rcv, c_snd, c_rcv, p_snd, p_rcv, q_snd, q_rcv, f_snd, f_rcv):
+           ids, cnt, coeff, domains, buf, w, fs, g, gs, rh, rl, lh, s0, s1, r0, r1, a0, a1, b0, b1, xs, xr, part, u0, u1, u2, v1, v2, v3,
+           i_sem, h_sem, l_sem, x_snd, x_rcv, c_snd, c_rcv, p_snd, p_rcv, q_snd, q_rcv, f_snd, f_rcv, e_snd, e_rcv):
     aux = lax.axis_index("aux")
     z = lax.axis_index("depth")
     x = lax.axis_index("blk")
@@ -104,7 +109,12 @@
     brow = lax.broadcasted_iota(jnp.int32, (64, 512), 0) % 4
     w[...] = jnp.where(brow == mu, wide, 0.0).astype(BF16)
 
-    x_copies, l_copies = [], []
+    def spread_over_x(t, h):
+        for d in (2, 1, 3):
+            send(fs.at[t, (x + d) % 4, h], g.at[t, x, h], x_snd, x_rcv.at[t, d - 1], at_x(d))
+        send(fs.at[t, x, h], gs.at[t, x, h], c_snd, c_rcv.at[t], sibling)
+        pltpu.make_async_copy(fs.at[t, x, h], g.at[t, x, h], l_sem.at[t]).start()
+
     for t in range(T):
         for h in range(2):
             loads[2 * t + h].wait()
@@ -121,50 +131,49 @@
                     for j in range(4):
                         for i in range(2):
                             r = 8 * j + 4 * i
-                            fs[t, j, i, pl.ds(8 * h + 2 * p + e, 4, stride=16), :] = res[r:r + 4, 128 * e:128 * e + 128]
+                            fs[t, j, h, i, pl.ds(2 * p + e, 4, stride=8), :] = res[r:r + 4, 128 * e:128 * e + 128]
                 return carry
 
             lax.fori_loop(0, 4, pair_of_m, 0)
-        if t == 0:
-            pl.semaphore_wait(barrier, 10)
-        for d in (2, 1, 3):
-            x_copies.append(send(fs.at[t, (x + d) % 4], g.at[t, x], x_snd, x_rcv.at[t, d - 1], at_x(d)))
-        send(fs.at[t, x], gs.at[t, x], c_snd, c_rcv.at[t], sibling)
-        cp = pltpu.make_async_copy(fs.at[t, x], g.at[t, x], l_sem.at[t])
-        cp.start()
-        l_copies.append(cp)
+            if t == h == 0:
+                pl.semaphore_wait(barrier, 10)
+            if t == 0:
+                spread_over_x(t, pl.ds(h, 1))
+        if t > 0:
+            spread_over_x(t, pl.ds(0, 2))
 
     def keep(src, t, k, base):
-        for i in range(2):
-            lanes = pl.ds(base + 128 * i, 128)
-            rows = pl.ds(pl.multiple_of(64 * k, 64), 64)
-            hi, lo = split(src[t, k, i])
-            rh[t, rows, lanes] = hi
-            rl[t, rows, lanes] = lo
-            hi, lo = split(src[t, k, i, pl.ds(pl.multiple_of(32 * c, 32), 32)])
-            lh[t, pl.ds(pl.multiple_of(32 * k, 32), 32), lanes] = hi
-            lh[t, pl.ds(pl.multiple_of(128 + 32 * k, 32), 32), lanes] = lo
+        for h in range(2):
+            for i in range(2):
+                lanes = pl.ds(base + 128 * i, 128)
+                rows = pl.ds(pl.multiple_of(64 * k + 32 * h, 32), 32)
+                hi, lo = split(src[t, k, h, i])
+                rh[t, rows, lanes] = hi
+                rl[t, rows, lanes] = lo
+                hi, lo = split(src[t, k, h, i, pl.ds(pl.multiple_of(16 * c, 16), 16)])
+                lh[t, pl.ds(pl.multiple_of(32 * k + 16 * h, 16), 16), lanes] = hi
+                lh[t, pl.ds(pl.multiple_of(128 + 32 * k + 16 * h, 16), 16), lanes] = lo
 
     con = ((1,), (1,))
 
     def store(res, at):
         for ky in range(4):
             for zz in range(4):
-                r = 32 * ky + 8 * zz
+                r = 32 * ky + 16 * (zz % 2) + 8 * (zz // 2)
                 s0[zz, at, ky] = res[r:r + 8, :128]
                 s1[ky, at, zz] = res[r:r + 8, 128:]
 
-    def columns(t):
-        big = dot(lh[:t].reshape(256 * t, 512), rh[t], con)
-        add = dot(jnp.concatenate([lh[u, :128] for u in range(t)], axis=0), rl[t], con)
-        for u in range(t):
-            res = big[256 * u:256 * u + 128] + big[256 * u + 128:256 * u + 256] + add[128 * u:128 * u + 128]
-            store(res, t * t + u)
-
-    def rows(t):
-        for u in range(t + 1):
-            big = dot(lh[t], rh[u], con)
-            store(big[:128] + big[128:] + dot(lh[t, :128], rl[u], con), t * t + t + u)
+    def columns(t, lanes):
+        big = dot(lh[:t, :, lanes].reshape(256 * t, 256), rh[t, :, lanes], con)
+        add = dot(jnp.concatenate([lh[u, :128, lanes] for u in range(t)], axis=0), rl[t, :, lanes], con)
+        return [big[256 * u:256 * u + 128] + big[256 * u + 128:256 * u + 256] + add[128 * u:128 * u + 128]
+                for u in range(t)]
+
+    def row(t, u, lanes):
+        big = dot(lh[t, :, lanes], rh[u, :, lanes], con)
+        return big[:128] + big[128:] + dot(lh[t, :128, lanes], rl[u, :, lanes], con)
+
+    mine, theirs = pl.ds(0, 256), pl.ds(256, 256)
 
     def first(k):
         n = pl.ds(*span(k))
@@ -183,55 +192,121 @@
             for d in (2, 1, 3):
                 send(a.at[(me + d) % 4, n], b.at[d - 1, n], q_snd.at[f], q_rcv.at[f, k], to(d))
 
-    ready = 0
+    def beside(t, u):
+        left, right = (part[v] + row(t, v, theirs) for v in (2 * u, 2 * u + 1))
+        half = lax.broadcasted_iota(jnp.int32, (128, 128), 1) < 64
+        for f in range(2):
+            even, odd = left[:, 128 * f:128 * f + 128], right[:, 128 * f:128 * f + 128]
+            for e, res in enumerate((
+                    jnp.where(half, even, pltpu.roll(odd, 64, axis=1)), jnp.where(half, pltpu.roll(even, 64, axis=1), odd))):
+                for ky in range(4):
+                    for zz in range(4):
+                        r = 32 * ky + 16 * (zz % 2) + 8 * (zz // 2)
+                        u0[2 * f + e, u, ky, zz] = res[r:r + 8]
+        for d in (2, 1, 3):
+            send(u0.at[(x + d) % 4, u], v1.at[d - 1, u], e_snd.at[0], e_rcv.at[0, u], at_x(d))
+
+    def beside_plane():
+        for u in range(2):
+            await_bytes(v1.at[:, u], e_rcv.at[0, u])
+            u1[:, :, u] = u0[x, u] + v1[0, u] + v1[1, u] + v1[2, u]
+        v2[4 * y + z] = u1[y, z]
+        for dy in (2, 1, 3, 0):
+            for dz in (2, 1, 3, 0):
+                if dy or dz:
+                    send(u1.at[(y + dy) % 4, (z + dz) % 4], v2.at[4 * y + z], e_snd.at[1], e_rcv.at[1, 0],
+                         {"aux": ((y + dy) % 4) * 2 + c, "depth": (z + dz) % 4})
+
+    def plane(k):
+        n = pl.ds(*span(k))
+        low = lax.broadcasted_iota(jnp.int32, (8, 128), 1) < 64
+        for f, (own, s, r) in enumerate(((z, s0, r0), (y, s1, r1))):
+            await_bytes(r.at[:, n], p_rcv.at[f, k])
+            tot = s[own, n] + r[0, n] + r[1, n] + r[2, n]
+            for v in range(4):
+                one, two, three = tot[0, v], tot[1, v], tot[2, v]
+                u2[f, v, 0, 0] = jnp.where(low, one, pltpu.roll(two, 64, axis=1))
+                u2[f, v, 1, 0] = jnp.where(low, pltpu.roll(one, 64, axis=1), two)
+                u2[f, v, 0, 1] = three
+                u2[f, v, 1, 1] = pltpu.roll(three, 64, axis=1)
+            me = (y, z)[f]
+            for e in range(2):
+                at = 2 * f + e
+                for d in (2, 1, 3):
+                    to = (y + d) % 4 if f == 0 else (z + d) % 4
+                    where = {"aux": to * 2 + c, "blk": at} if f == 0 else {"depth": to, "blk": at}
+                    send(u2.at[f, to, e], v3.at[4 * me + x], e_snd.at[2], e_rcv.at[2, 0], where)
+
+                @pl.when(x != at)
+                def _(f=f, e=e, at=at, me=me):
+                    send(u2.at[f, me, e], v3.at[4 * me + x], e_snd.at[2], e_rcv.at[2, 0], {"blk": at})
+
+        flow = x // 2
+        me = y + flow * (z - y)
+        v3[4 * me + x] = u2[flow, me, x % 2]
+
     for t in range(T):
-        l_copies[t].wait()
+        pltpu.make_async_copy(fs.at[t, 0], g.at[t, 0], l_sem.at[t]).wait()
         keep(g, t, x, 0)
         for d in (1, 3, 2):
-            x_copies[3 * t + (2, 1, 3).index(d)].wait_recv()
             k = (x - d + 4) % 4
+            await_bytes(g.at[t, k], x_rcv.at[t, d - 1])
             send(g.at[t, k], gs.at[t, k], c_snd, c_rcv.at[t], sibling)
             keep(g, t, k, 0)
+        for u in range(t + 1):
+            part[u] = row(t, u, mine)
+        if t > 0:
+            for u, res in enumerate(columns(t, mine)):
+                part[T + u] = res
         await_bytes(gs.at[t], c_rcv.at[t])
         for k in range(4):
             keep(gs, t, k, 256)
+        if t == T - 1:
+            beside(t, 0)
+        else:
+            for u in range(t + 1):
+                store(part[u] + row(t, u, theirs), PLACE[t, u])
         if t > 0:
-            columns(t)
+            for u, res in enumerate(columns(t, theirs)):
+                store(part[T + u] + res, PLACE[u, t])
+        first(t)
         if t == T - 1:
-            first(3)
-        rows(t)
-        first(min(t, 3) + (t == T - 1))
-        if t > 0:
-            second(t - 1)
-    second(3)
-    second(4)
-
-    done = []
+            beside(t, 1)
+        if t == 2:
+            second(0)
+    second(1)
+    second(2)
+    beside_plane()
+    plane(3)
+
+    low = lax.broadcasted_iota(jnp.int32, (8, 128), 1) < 64
+
     for f, (a, b, me) in enumerate(((a0, b0, y), (a1, b1, z))):
-        for k in range(len(GROUPS)):
+        for k in STEPWISE:
             await_bytes(b.at[:, pl.ds(*span(k))], q_rcv.at[f, k])
-        done.append(a[me] + b[0] + b[1] + b[2])
-
-    def place(tr, tc):
-        return tr * tr + tr + tc if tr >= tc else tc * tc + tr
-
-    for f in range(2):
-        for tr in range(T):
-            for u in range(2):
-                even, odd = done[f][place(tr, 2 * u)], done[f][place(tr, 2 * u + 1)]
-                xs[2 * f, tr, u] = jnp.where(low, even, pltpu.roll(odd, 64, axis=1))
-                xs[2 * f + 1, tr, u] = jnp.where(low, pltpu.roll(even, 64, axis=1), odd)
+        for at, pair in enumerate(PAIRS):
+            even, odd = (a[me, p] + b[0, p] + b[1, p] + b[2, p] for p in (PLACE[pair[0]], PLACE[pair[-1]]))
+            xs[2 * f, at] = jnp.where(low, even, pltpu.roll(odd, 64, axis=1))
+            xs[2 * f + 1, at] = jnp.where(low, pltpu.roll(even, 64, axis=1), odd)
     for d in (2, 1, 3):
         send(xs.at[(x + d) % 4], xr.at[d - 1], f_snd, f_rcv, at_x(d))
     await_bytes(xr, f_rcv)
-    total = xs[x] + xr[0] + xr[1] + xr[2]
+    sums = xs[x] + xr[0] + xr[1] + xr[2]
+    await_bytes(v2.at[pl.ds(0, 15)], e_rcv.at[1, 0])
+    rows_3 = jnp.sum(v2[...], axis=0)
+    await_bytes(v3.at[pl.ds(0, 15)], e_rcv.at[2, 0])
+    cols_3 = jnp.sum(v3[...], axis=0)
+    total = {(0, 0): sums[0], (1, 0): sums[1], (2, 0): sums[2], (3, 0): rows_3[0], (3, 1): rows_3[1]}
+    total[0, 1] = jnp.where(low, sums[3], pltpu.roll(cols_3[0], 64, axis=1))
+    total[1, 1] = jnp.where(low, pltpu.roll(sums[3], 64, axis=1), cols_3[0])
+    total[2, 1] = jnp.where(low, sums[4], pltpu.roll(cols_3[1], 64, axis=1))
     pieces = {}
     for u in range(2):
-        turned = total[:, u].reshape(32, 128).T
+        turned = jnp.concatenate([total[tr, u] for tr in range(T)], axis=0).T
         for e in range(2):
             for b in range(4):
                 for h in range(2):
-                    r = 64 * e + 16 * b + 8 * h
+                    r = 64 * e + 32 * h + 8 * b
                     pieces[b, h, 2 * u + e] = turned[r:r + 8]
     for half in range(2):
         cols = jnp.concatenate([pieces[k] for k in sorted(pieces) if k[0] // 2 == half], axis=0)
@@ -242,6 +317,9 @@
         await_bytes(r, p_snd.at[f])
         await_bytes(b, q_snd.at[f])
     await_bytes(xr, f_snd)
+    await_bytes(v1, e_snd.at[0])
+    await_bytes(v2.at[pl.ds(0, 15)], e_snd.at[1])
+    await_bytes(v3.at[pl.ds(0, 15)], e_snd.at[2])
 
 
 def hold(v):
@@ -261,28 +339,31 @@
             vmem((1, 8), jnp.int32), vmem((1, 1), jnp.int32), vmem((8, 1024), F32), vmem((8, 24), jnp.int32),
             vmem((8, 64, 64, 128), F32),
             vmem((64, 512), BF16),
-            vmem((T, 4, 2, 64, 128), F32),
-            vmem((T, 4, 2, 64, 128), F32),
-            vmem((T, 4, 2, 64, 128), F32),
+            vmem((T, 4, 2, 2, 32, 128), F32),
+            vmem((T, 4, 2, 2, 32, 128), F32),
+            vmem((T, 4, 2, 2, 32, 128), F32),
             vmem((T, 256, 512), BF16),
             vmem((T, 256, 512), BF16),
             vmem((T, 256, 512), BF16),
-            vmem((4, 16, 4, 8, 128), F32),
-            vmem((4, 16, 4, 8, 128), F32),
-            vmem((3, 16, 4, 8, 128), F32),
-            vmem((3, 16, 4, 8, 128), F32),
-            vmem((4, 16, 8, 128), F32),
-            vmem((4, 16, 8, 128), F32),
-            vmem((3, 16, 8, 128), F32),
-            vmem((3, 16, 8, 128), F32),
-            vmem((4, 4, 2, 8, 128), F32),
-            vmem((3, 4, 2, 8, 128), F32),
+            vmem((4, NB, 4, 8, 128), F32),
+            vmem((4, NB, 4, 8, 128), F32),
+            vmem((3, NB, 4, 8, 128), F32),
+            vmem((3, NB, 4, 8, 128), F32),
+            vmem((4, NQ, 8, 128), F32),
+            vmem((4, NQ, 8, 128), F32),
+            vmem((3, NQ, 8, 128), F32),
+            vmem((3, NQ, 8, 128), F32),
+            vmem((4, len(PAIRS), 8, 128), F32),
+            vmem((3, len(PAIRS), 8, 128), F32),
+            vmem((2 * T - 1, 128, 256), F32),
+            vmem((4, 2, 4, 4, 8, 128), F32), vmem((4, 4, 2, 8, 128), F32), vmem((2, 4, 2, 2, 8, 128), F32),
+            vmem((3, 2, 4, 4, 8, 128), F32), vmem((16, 2, 8, 128), F32), vmem((16, 2, 8, 128), F32),
             dma((4,)), dma((T, 2)), dma((T,)),
             dma, dma((T, 3)),
             dma, dma((T,)),
             dma((2,)), dma((2, len(GROUPS))),
             dma((2,)), dma((2, len(GROUPS))),
-            dma, dma,
+            dma, dma, dma((3,)), dma((3, 2)),
         ],
         compiler_params=pltpu.CompilerParams(
             collective_id=0, has_side_effects=True, vmem_limit_bytes=VMEM_LIMIT),

time: 43.4 us -> 38.1 us (0.88)
  Pallas kernels: 42.1 us -> 36.7 us
    pallas_call x1, Pallas kernels: 42.1 us -> 36.7 us  [on_device(): pl.pallas_call(kernel, out_shape=jax.ShapeDtypeStruct((32, 256), F32), in...]
where the time goes in v3:
time: 38.1 us; the launch traced here: 38 us
  Pallas kernels  36.7 us (96%)
  between operations  0.66 us (2%)
  local copies, waits for them, and re-layouts  0.62 us (2%)
    pallas_call x1, Pallas kernels, on_device(): pl.pallas_call(kernel, out_shape=jax.ShapeDtypeStruct((32, 256), F32), in...  36.7 us

profile of v3, /device:TPU:0, one launch (start us, length us, event | category | flops | bytes accessed | tf_op | source)
XLA Modules:
  0.0 38.0 jit_solution(6431468626949330416)
XLA Ops:
  0.7 36.7 %shard_map.55 = f32[32,256]{1,0:T(8,128)S(1)} custom-call(s32[1,8]{1,0:T(1,128)} %ids_in.1, s32[1,1]{1,0:T(1,128)S(6)} %copy.7.cnt_in, f32[8,1024]{1,0:T(8,128)} %coeff_in.1, s32[8,24]{1,0:T(8,128)} %domains_in.1, f32[1,8,64,64,128]{4,3,2,1,0:T(8,128)} %blocks.1), custom_call_target="tpu_custom_call" | custom-call | tf_op jit(solution)/shard_map/pallas_call | solution.py:333
  37.4 0.6 %copy.8 = f32[256,32]{0,1:T(8,128)} copy(f32[256,32]{0,1:T(8,128)S(1)} %bitcast.1) | data formatting | bytes 65536

commit v4 on v3

--- a/solution.py
+++ b/solution.py
@@ -13,7 +13,7 @@
     ((0, 0),),
     ((0, 1), (1, 0), (1, 1)),
     ((0, 2), (1, 2), (2, 0), (2, 1), (2, 2)),
-    ((0, 3), (1, 3), (2, 3)),
+    ((0, 3), (1, 3), (2, 3), (3, 3)),
 )
 PLACE = {pair: at for at, pair in enumerate(sum(GROUPS, ()))}
 NB = len(PLACE)
@@ -36,7 +36,7 @@
 
 
 def kernel(ids_in, cnt_in, coeff_in, domains_in, blocks, out,
-           ids, cnt, coeff, domains, buf, w, fs, g, gs, rh, rl, lh, s0, s1, r0, r1, a0, a1, b0, b1, xs, xr, part, u0, u1, u2, v1, v2, v3,
+           ids, cnt, coeff, domains, buf, w, fs, g, gs, rh, rl, lh, s0, s1, r0, r1, a0, a1, b0, b1, xs, xr, part, u0, u1, u2, u3, v1, v2, v3, v4,
            i_sem, h_sem, l_sem, x_snd, x_rcv, c_snd, c_rcv, p_snd, p_rcv, q_snd, q_rcv, f_snd, f_rcv, e_snd, e_rcv):
     aux = lax.axis_index("aux")
     z = lax.axis_index("depth")
@@ -134,7 +134,7 @@
                             fs[t, j, h, i, pl.ds(2 * p + e, 4, stride=8), :] = res[r:r + 4, 128 * e:128 * e + 128]
                 return carry
 
-            lax.fori_loop(0, 4, pair_of_m, 0)
+            lax.fori_loop(0, 4, pair_of_m, 0, unroll=4 if t == h == 0 else 1)
             if t == h == 0:
                 pl.semaphore_wait(barrier, 10)
             if t == 0:
@@ -192,24 +192,30 @@
             for d in (2, 1, 3):
                 send(a.at[(me + d) % 4, n], b.at[d - 1, n], q_snd.at[f], q_rcv.at[f, k], to(d))
 
-    def beside(t, u):
-        left, right = (part[v] + row(t, v, theirs) for v in (2 * u, 2 * u + 1))
-        half = lax.broadcasted_iota(jnp.int32, (128, 128), 1) < 64
+    def beside(pair):
+        cols = (0, 1) if pair else (2,)
+        res = [part[u] + row(T - 1, u, theirs) for u in cols]
+        n = 128 if pair else 64
+        half = lax.broadcasted_iota(jnp.int32, (n, 128), 1) < 64
+        dst, got = (u0, v1) if pair else (u3, v4)
         for f in range(2):
-            even, odd = left[:, 128 * f:128 * f + 128], right[:, 128 * f:128 * f + 128]
-            for e, res in enumerate((
+            even, odd = res[0][:n, 128 * f:128 * f + 128], res[-1][128 - n:, 128 * f:128 * f + 128]
+            for e, both in enumerate((
                     jnp.where(half, even, pltpu.roll(odd, 64, axis=1)), jnp.where(half, pltpu.roll(even, 64, axis=1), odd))):
-                for ky in range(4):
+                for ky in range(n // 32):
                     for zz in range(4):
                         r = 32 * ky + 16 * (zz % 2) + 8 * (zz // 2)
-                        u0[2 * f + e, u, ky, zz] = res[r:r + 8]
+                        dst[2 * f + e, ky, zz] = both[r:r + 8]
         for d in (2, 1, 3):
-            send(u0.at[(x + d) % 4, u], v1.at[d - 1, u], e_snd.at[0], e_rcv.at[0, u], at_x(d))
+            send(dst.at[(x + d) % 4], got.at[d - 1], e_snd.at[0], e_rcv.at[0, 1 - pair], at_x(d))
 
     def beside_plane():
-        for u in range(2):
-            await_bytes(v1.at[:, u], e_rcv.at[0, u])
-            u1[:, :, u] = u0[x, u] + v1[0, u] + v1[1, u] + v1[2, u]
+        await_bytes(v1, e_rcv.at[0, 0])
+        u1[:, :, 0] = u0[x] + v1[0] + v1[1] + v1[2]
+        await_bytes(v4, e_rcv.at[0, 1])
+        tot = u3[x] + v4[0] + v4[1] + v4[2]
+        u1[:2, :, 1] = tot
+        u1[2:, :, 1] = pltpu.roll(tot.reshape(64, 128), 64, axis=1).reshape(2, 4, 8, 128)
         v2[4 * y + z] = u1[y, z]
         for dy in (2, 1, 3, 0):
             for dz in (2, 1, 3, 0):
@@ -224,11 +230,10 @@
             await_bytes(r.at[:, n], p_rcv.at[f, k])
             tot = s[own, n] + r[0, n] + r[1, n] + r[2, n]
             for v in range(4):
-                one, two, three = tot[0, v], tot[1, v], tot[2, v]
-                u2[f, v, 0, 0] = jnp.where(low, one, pltpu.roll(two, 64, axis=1))
-                u2[f, v, 1, 0] = jnp.where(low, pltpu.roll(one, 64, axis=1), two)
-                u2[f, v, 0, 1] = three
-                u2[f, v, 1, 1] = pltpu.roll(three, 64, axis=1)
+                for e in range(2):
+                    one, two = tot[2 * e, v], tot[2 * e + 1, v]
+                    u2[f, v, 0, e] = jnp.where(low, one, pltpu.roll(two, 64, axis=1))
+                    u2[f, v, 1, e] = jnp.where(low, pltpu.roll(one, 64, axis=1), two)
             me = (y, z)[f]
             for e in range(2):
                 at = 2 * f + e
@@ -262,16 +267,18 @@
         for k in range(4):
             keep(gs, t, k, 256)
         if t == T - 1:
-            beside(t, 0)
+            beside(1)
         else:
             for u in range(t + 1):
                 store(part[u] + row(t, u, theirs), PLACE[t, u])
         if t > 0:
             for u, res in enumerate(columns(t, theirs)):
                 store(part[T + u] + res, PLACE[u, t])
+        if t == T - 1:
+            store(part[t] + row(t, t, theirs), PLACE[t, t])
         first(t)
         if t == T - 1:
-            beside(t, 1)
+            beside(0)
         if t == 2:
             second(0)
     second(1)
@@ -296,10 +303,11 @@
     rows_3 = jnp.sum(v2[...], axis=0)
     await_bytes(v3.at[pl.ds(0, 15)], e_rcv.at[2, 0])
     cols_3 = jnp.sum(v3[...], axis=0)
-    total = {(0, 0): sums[0], (1, 0): sums[1], (2, 0): sums[2], (3, 0): rows_3[0], (3, 1): rows_3[1]}
+    total = {(0, 0): sums[0], (1, 0): sums[1], (2, 0): sums[2], (3, 0): rows_3[0]}
     total[0, 1] = jnp.where(low, sums[3], pltpu.roll(cols_3[0], 64, axis=1))
     total[1, 1] = jnp.where(low, pltpu.roll(sums[3], 64, axis=1), cols_3[0])
     total[2, 1] = jnp.where(low, sums[4], pltpu.roll(cols_3[1], 64, axis=1))
+    total[3, 1] = jnp.where(low, rows_3[1], cols_3[1])
     pieces = {}
     for u in range(2):
         turned = jnp.concatenate([total[tr, u] for tr in range(T)], axis=0).T
@@ -318,6 +326,7 @@
         await_bytes(b, q_snd.at[f])
     await_bytes(xr, f_snd)
     await_bytes(v1, e_snd.at[0])
+    await_bytes(v4, e_snd.at[0])
     await_bytes(v2.at[pl.ds(0, 15)], e_snd.at[1])
     await_bytes(v3.at[pl.ds(0, 15)], e_snd.at[2])
 
@@ -356,8 +365,10 @@
             vmem((4, len(PAIRS), 8, 128), F32),
             vmem((3, len(PAIRS), 8, 128), F32),
             vmem((2 * T - 1, 128, 256), F32),
-            vmem((4, 2, 4, 4, 8, 128), F32), vmem((4, 4, 2, 8, 128), F32), vmem((2, 4, 2, 2, 8, 128), F32),
-            vmem((3, 2, 4, 4, 8, 128), F32), vmem((16, 2, 8, 128), F32), vmem((16, 2, 8, 128), F32),
+            vmem((4, 4, 4, 8, 128), F32), vmem((4, 4, 2, 8, 128), F32), vmem((2, 4, 2, 2, 8, 128), F32),
+            vmem((4, 2, 4, 8, 128), F32),
+            vmem((3, 4, 4, 8, 128), F32), vmem((16, 2, 8, 128), F32), vmem((16, 2, 8, 128), F32),
+            vmem((3, 2, 4, 8, 128), F32),
             dma((4,)), dma((T, 2)), dma((T,)),
             dma, dma((T, 3)),
             dma, dma((T,)),

time: 38.1 us -> 36.8 us (0.966)
  Pallas kernels: 36.7 us -> 35.3 us
    pallas_call x1, Pallas kernels: 36.7 us -> 35.3 us  [on_device(): pl.pallas_call(kernel, out_shape=jax.ShapeDtypeStruct((32, 256), F32), in...]
where the time goes in v4:
time: 36.8 us; the launch traced here: 36.6 us
  Pallas kernels  35.3 us (96%)
  between operations  0.66 us (2%)
  local copies, waits for them, and re-layouts  0.62 us (2%)
    pallas_call x1, Pallas kernels, on_device(): pl.pallas_call(kernel, out_shape=jax.ShapeDtypeStruct((32, 256), F32), in...  35.3 us

profile of v4, /device:TPU:0, one launch (start us, length us, event | category | flops | bytes accessed | tf_op | source)
XLA Modules:
  0.0 36.6 jit_solution(834575173020551948)
XLA Ops:
  0.7 35.3 %shard_map.55 = f32[32,256]{1,0:T(8,128)S(1)} custom-call(s32[1,8]{1,0:T(1,128)} %ids_in.1, s32[1,1]{1,0:T(1,128)S(6)} %copy.7.cnt_in, f32[8,1024]{1,0:T(8,128)} %coeff_in.1, s32[8,24]{1,0:T(8,128)} %domains_in.1, f32[1,8,64,64,128]{4,3,2,1,0:T(8,128)} %blocks.1), custom_call_target="tpu_custom_call" | custom-call | tf_op jit(solution)/shard_map/pallas_call | solution.py:342
  35.9 0.6 %copy.8 = f32[256,32]{0,1:T(8,128)} copy(f32[256,32]{0,1:T(8,128)S(1)} %bitcast.1) | data formatting | bytes 65536

commit v5 on v4

--- a/solution.py
+++ b/solution.py
@@ -109,11 +109,13 @@
     brow = lax.broadcasted_iota(jnp.int32, (64, 512), 0) % 4
     w[...] = jnp.where(brow == mu, wide, 0.0).astype(BF16)
 
+    kept = pl.ds(0, 32)
+
     def spread_over_x(t, h):
         for d in (2, 1, 3):
-            send(fs.at[t, (x + d) % 4, h], g.at[t, x, h], x_snd, x_rcv.at[t, d - 1], at_x(d))
-        send(fs.at[t, x, h], gs.at[t, x, h], c_snd, c_rcv.at[t], sibling)
-        pltpu.make_async_copy(fs.at[t, x, h], g.at[t, x, h], l_sem.at[t]).start()
+            send(fs.at[t, (x + d) % 4, h, :, kept], g.at[t, x, h], x_snd, x_rcv.at[t, d - 1], at_x(d))
+        send(fs.at[t, x, h, :, kept], gs.at[t, x, h], c_snd, c_rcv.at[t], sibling)
+        pltpu.make_async_copy(fs.at[t, x, h, :, kept], g.at[t, x, h], l_sem.at[t]).start()
 
     for t in range(T):
         for h in range(2):
@@ -235,12 +237,16 @@
                     u2[f, v, 0, e] = jnp.where(low, one, pltpu.roll(two, 64, axis=1))
                     u2[f, v, 1, e] = jnp.where(low, pltpu.roll(one, 64, axis=1), two)
             me = (y, z)[f]
+            for d in (2, 1, 3):
+                to = (y + d) % 4 if f == 0 else (z + d) % 4
+                for e in range(2):
+                    at = 2 * f + e
+                    where = {"aux": to * 2 + c, "blk": at} if f == 0 else {"depth": to, "blk": at}
+                    send(u2.at[f, to, e], v3.at[4 * me + x], e_snd.at[2], e_rcv.at[2, 0], where)
+        for f in range(2):
+            me = (y, z)[f]
             for e in range(2):
                 at = 2 * f + e
-                for d in (2, 1, 3):
-                    to = (y + d) % 4 if f == 0 else (z + d) % 4
-                    where = {"aux": to * 2 + c, "blk": at} if f == 0 else {"depth": to, "blk": at}
-                    send(u2.at[f, to, e], v3.at[4 * me + x], e_snd.at[2], e_rcv.at[2, 0], where)
 
                 @pl.when(x != at)
                 def _(f=f, e=e, at=at, me=me):
@@ -251,7 +257,7 @@
         v3[4 * me + x] = u2[flow, me, x % 2]
 
     for t in range(T):
-        pltpu.make_async_copy(fs.at[t, 0], g.at[t, 0], l_sem.at[t]).wait()
+        await_bytes(g.at[t, 0], l_sem.at[t])
         keep(g, t, x, 0)
         for d in (1, 3, 2):
             k = (x - d + 4) % 4
@@ -319,7 +325,7 @@
     for half in range(2):
         cols = jnp.concatenate([pieces[k] for k in sorted(pieces) if k[0] // 2 == half], axis=0)
         out[:, 128 * half:128 * half + 128] = cols.T
-    await_bytes(fs.at[:, :3], x_snd)
+    await_bytes(g.at[:, :3], x_snd)
     await_bytes(gs, c_snd)
     for f, (r, b) in enumerate(((r0, b0), (r1, b1))):
         await_bytes(r, p_snd.at[f])
@@ -348,7 +354,7 @@
             vmem((1, 8), jnp.int32), vmem((1, 1), jnp.int32), vmem((8, 1024), F32), vmem((8, 24), jnp.int32),
             vmem((8, 64, 64, 128), F32),
             vmem((64, 512), BF16),
-            vmem((T, 4, 2, 2, 32, 128), F32),
+            vmem((T, 4, 2, 2, 40, 128), F32),
             vmem((T, 4, 2, 2, 32, 128), F32),
             vmem((T, 4, 2, 2, 32, 128), F32),
             vmem((T, 256, 512), BF16),

time: 36.8 us -> 36.8 us (level)
  no operation moved by 1% of the time
where the time goes in v5:
time: 36.8 us; the launch traced here: 36.5 us
  Pallas kernels  35.2 us (96%)
  between operations  0.66 us (2%)
  local copies, waits for them, and re-layouts  0.62 us (2%)
    pallas_call x1, Pallas kernels, on_device(): pl.pallas_call(kernel, out_shape=jax.ShapeDtypeStruct((32, 256), F32), in...  35.2 us

profile of v5, /device:TPU:0, one launch (start us, length us, event | category | flops | bytes accessed | tf_op | source)
XLA Modules:
  0.0 36.5 jit_solution(14106357875726493754)
XLA Ops:
  0.7 35.2 %shard_map.55 = f32[32,256]{1,0:T(8,128)S(1)} custom-call(s32[1,8]{1,0:T(1,128)} %ids_in.1, s32[1,1]{1,0:T(1,128)S(6)} %copy.7.cnt_in, f32[8,1024]{1,0:T(8,128)} %coeff_in.1, s32[8,24]{1,0:T(8,128)} %domains_in.1, f32[1,8,64,64,128]{4,3,2,1,0:T(8,128)} %blocks.1), custom_call_target="tpu_custom_call" | custom-call | tf_op jit(solution)/shard_map/pallas_call | solution.py:348
  35.9 0.6 %copy.8 = f32[256,32]{0,1:T(8,128)} copy(f32[256,32]{0,1:T(8,128)S(1)} %bitcast.1) | data formatting | bytes 65536

commit v6 on v5

--- a/solution.py
+++ b/solution.py
@@ -285,8 +285,7 @@
         first(t)
         if t == T - 1:
             beside(0)
-        if t == 2:
-            second(0)
+    second(0)
     second(1)
     second(2)
     beside_plane()

time: 36.8 us -> 36.6 us (level)
  no operation moved by 1% of the time
where the time goes in v6:
time: 36.6 us; the launch traced here: 36.3 us
  Pallas kernels  35 us (96%)
  between operations  0.66 us (2%)
  local copies, waits for them, and re-layouts  0.62 us (2%)
    pallas_call x1, Pallas kernels, on_device(): pl.pallas_call(kernel, out_shape=jax.ShapeDtypeStruct((32, 256), F32), in...  35 us

profile of v6, /device:TPU:0, one launch (start us, length us, event | category | flops | bytes accessed | tf_op | source)
XLA Modules:
  0.0 36.3 jit_solution(8482718994673802703)
XLA Ops:
  0.7 35.0 %shard_map.55 = f32[32,256]{1,0:T(8,128)S(1)} custom-call(s32[1,8]{1,0:T(1,128)} %ids_in.1, s32[1,1]{1,0:T(1,128)S(6)} %copy.7.cnt_in, f32[8,1024]{1,0:T(8,128)} %coeff_in.1, s32[8,24]{1,0:T(8,128)} %domains_in.1, f32[1,8,64,64,128]{4,3,2,1,0:T(8,128)} %blocks.1), custom_call_target="tpu_custom_call" | custom-call | tf_op jit(solution)/shard_map/pallas_call | solution.py:347
  35.6 0.6 %copy.8 = f32[256,32]{0,1:T(8,128)} copy(f32[256,32]{0,1:T(8,128)S(1)} %bitcast.1) | data formatting | bytes 65536
